TPU v7x, 512 devices: a whole 4x4x16 slice. The times are simulated.
512 devices in a mesh: seq: 64 (over z, x), head: 2 (over core), dp: 4 (over y).
Axes of the slice: x: 4, y: 4, z: 16, core: 2. Of those that a mesh axis runs over, the one named last changes fastest.
Arguments:
- hidden: bfloat16 [4, 12288, 1024], P('dp', 'seq'), may hold values from -6 to 6
- norm_gain: float32 [1024], replicated, may hold values from 0.5 to 1.5
- projection: bfloat16 [3, 1024, 1024], P(None, None, 'head'), may hold values from -1 to 1
- upstream: bfloat16 [4, 12288, 1024], P('dp', 'seq', 'head'), may hold values from -6 to 6
- cluster: int32 [4, 12288, 1], P('dp', 'seq'), may hold values from 0 to 63; in each aligned block of 192 rows (0 to 191, 192 to 383, ..., all dimensions but the last counted through in order) at most 9 rows name the same one
Outputs:
- input_gradient: bfloat16 [4, 12288, 1024], P('dp', 'seq', 'head')
- gain_gradient: float32 [1024], P('head')
Inputs may be any that keep to these rules, and one draw needn't show every extreme that they name: Among the 192 tokens of one device no cluster is named more than 9 times, a bound that some block reaches.
All inputs are finite; a program needn't handle non-finite values.
Results may differ from a plain program's by a relative error of at most 0.01.
The roundings to bfloat16 on the way count: a program that leaves them out, or rounds other values in their place, can miss the bound.
Values may be sent and summed in bfloat16 or wider, within the bound.
No kernel may reach another device: no remote copies, remote signals or barrier semaphores. Data moves between devices by JAX's collectives and lax.ppermute only.
A program may use at most 64 MiB of HBM per device.

v0:
```python
import jax
import jax.numpy as jnp
from jax import lax
from jax.sharding import PartitionSpec as P

HDIM = 64
CLUS_DEV = 1
epsilon = 1e-05
masked = -1e30


def normalize(values, norm_gain):
    values = values.astype(jnp.float32)
    center = values - jnp.mean(values, -1, keepdims=True)
    spread = lax.rsqrt(jnp.mean(center * center, -1, keepdims=True) + epsilon)
    scaled = center * spread
    return (scaled, spread, (scaled * norm_gain).astype(jnp.bfloat16))


def attend_backward(queries, key_rows, values, upstream, allowed, factor):
    scores = (
        lax.dot_general(
            queries, key_rows, (((1,), (1,)), ((), ())), preferred_element_type=jnp.float32
        )
        * factor
    )
    scores = jnp.where(allowed, scores, masked)
    powers = jnp.exp(scores - jnp.max(scores, -1, keepdims=True))
    weights = powers / jnp.sum(powers, -1, keepdims=True)
    rounded = weights.astype(jnp.bfloat16)
    output = jnp.dot(rounded, values, preferred_element_type=jnp.float32)
    center_term = jnp.sum(upstream.astype(jnp.float32) * output, -1, keepdims=True)
    grad_values = lax.dot_general(
        rounded, upstream, (((0,), (0,)), ((), ())), preferred_element_type=jnp.float32
    ).astype(jnp.bfloat16)
    grad_weights = lax.dot_general(
        upstream, values, (((1,), (1,)), ((), ())), preferred_element_type=jnp.float32
    )
    grad_scores = (weights * (grad_weights - center_term) * factor).astype(jnp.bfloat16)
    grad_queries = jnp.dot(grad_scores, key_rows, preferred_element_type=jnp.float32).astype(
        jnp.bfloat16
    )
    grad_keys = lax.dot_general(
        grad_scores, queries, (((0,), (0,)), ((), ())), preferred_element_type=jnp.float32
    ).astype(jnp.bfloat16)
    return (grad_queries, grad_keys, grad_values)


def cluster_grads(payload, validity, head_width):
    row_count = payload.shape[0]
    spans = payload.shape[1] // 4
    heads_local = spans // head_width
    positions = lax.broadcasted_iota(jnp.int32, (row_count, row_count), 0)
    others = lax.broadcasted_iota(jnp.int32, (row_count, row_count), 1)
    allowed = (positions >= others) & (validity[None, :] > 0)
    factor = head_width ** (-0.5)

    def one_head(head_index, result):
        offset = head_index * head_width

        def select(portion):
            return lax.dynamic_slice_in_dim(payload, portion * spans + offset, head_width, 1)

        grads_head = attend_backward(select(0), select(1), select(2), select(3), allowed, factor)
        for portion in range(3):
            result = lax.dynamic_update_slice_in_dim(
                result, grads_head[portion], portion * spans + offset, 1
            )
        return result

    return lax.fori_loop(0, heads_local, one_head, jnp.zeros((row_count, 3 * spans), jnp.bfloat16))


def on_device(hidden, norm_gain, projection, upstream, cluster):
    seq_count = lax.axis_size("seq")
    tokens = hidden.shape[1]
    width_model = hidden.shape[2]
    spans = projection.shape[2]
    clusters_all = CLUS_DEV * seq_count
    slot_rows = 3 * tokens // clusters_all
    scaled, spread, normed = normalize(hidden[0], norm_gain)
    labels = cluster[0, :, 0]
    member = (labels[:, None] == jnp.arange(clusters_all, dtype=jnp.int32)[None, :]).astype(
        jnp.int32
    )
    ranks = jnp.sum(jnp.cumsum(member, 0) * member, 1) - 1
    target = labels * slot_rows + ranks
    projected = jnp.einsum(
        "td,kdh->tkh", normed, projection, preferred_element_type=jnp.float32
    ).astype(jnp.bfloat16)
    payload = jnp.concatenate([projected.reshape(tokens, 3 * spans), upstream[0]], 1)
    columns = payload.shape[1]
    outgoing = jnp.zeros((clusters_all * slot_rows, columns), jnp.bfloat16).at[target].set(payload)
    outgoing = outgoing.reshape(seq_count, CLUS_DEV, slot_rows, columns)
    present = jnp.zeros((clusters_all * slot_rows,), jnp.bfloat16).at[target].set(1.0)
    present = present.reshape(seq_count, CLUS_DEV, slot_rows)
    rows_in = lax.all_to_all(outgoing, "seq", split_axis=0, concat_axis=0, tiled=True)
    marks_in = lax.all_to_all(present, "seq", split_axis=0, concat_axis=0, tiled=True)
    sources = rows_in.shape[0]
    item_count = rows_in.shape[1]
    stacked = jnp.swapaxes(rows_in, 0, 1).reshape(item_count, sources * slot_rows, rows_in.shape[3])
    mark_rows = jnp.swapaxes(marks_in, 0, 1).reshape(item_count, sources * slot_rows)

    def per_item(entries):
        return cluster_grads(entries[0], entries[1].astype(jnp.float32), HDIM)

    results = lax.map(per_item, (stacked, mark_rows))
    width_out = results.shape[-1]
    results = results.reshape(item_count, sources, slot_rows, width_out)
    answer = jnp.swapaxes(results, 0, 1)
    returned = lax.all_to_all(answer, "seq", split_axis=0, concat_axis=0, tiled=True)
    restored = returned.reshape(clusters_all * slot_rows, 3 * spans)[target]
    partial_value = jnp.einsum(
        "tkh,kdh->td",
        restored.reshape(tokens, 3, spans),
        projection,
        preferred_element_type=jnp.float32,
    )
    partial_value = lax.optimization_barrier(partial_value.astype(jnp.bfloat16)).astype(jnp.float32)
    half_width = width_model // lax.axis_size("head")
    offset = lax.axis_index("head") * half_width
    own_scaled = lax.dynamic_slice_in_dim(scaled, offset, half_width, 1)
    own_gain = lax.dynamic_slice_in_dim(norm_gain, offset, half_width, 0)
    gradient = lax.psum_scatter(
        partial_value.astype(jnp.bfloat16), "head", scatter_dimension=1, tiled=True
    ).astype(jnp.float32)
    scaled_grad = gradient * own_gain
    first_sum, second_sum = lax.psum(
        (
            jnp.sum(scaled_grad, -1, keepdims=True),
            jnp.sum(scaled_grad * own_scaled, -1, keepdims=True),
        ),
        "head",
    )
    first_mean = first_sum / width_model
    second_mean = second_sum / width_model
    input_gradient = (spread * (scaled_grad - first_mean - own_scaled * second_mean)).astype(
        jnp.bfloat16
    )
    local_sum = jnp.sum(gradient * own_scaled, 0)
    gain_total = lax.psum(local_sum, ("seq", "dp"))
    gain_gradient = gain_total * (seq_count * lax.axis_size("dp") * tokens) ** (-0.5)
    return (input_gradient.reshape(1, tokens, half_width), gain_gradient)


def solution(mesh):
    in_specs = (
        P("dp", "seq", None),
        P(),
        P(None, None, "head"),
        P("dp", "seq", "head"),
        P("dp", "seq", None),
    )
    out_specs = (P("dp", "seq", "head"), P("head"))
    return jax.shard_map(
        on_device, mesh=mesh, in_specs=in_specs, out_specs=out_specs, check_vma=False
    )
```

profile of v0, /device:TPU:1, one launch (start us, length us, event | category | flops | bytes accessed | tf_op | source)
XLA Modules:
  0.0 1259.5 jit_solution(10916248163489631353)
XLA Ops:
  10.4 1.8 scatter_custom_fusion.1
  12.9 19.1 %all-to-all-start.1 = ((bf16[64,1,9]{2,1,0:T(2,128)(2,1)}), bf16[64,1,9]{2,1,0:T(2,128)(2,1)S(1)}, u32[]{:S(2)}, u32[]{:S(2)}) async-start(bf16[64,1,9]{2,1,0:T(2,128)(2,1)} %reshape.133), calls=%async_computation.1 | async-start | bytes 65536 | tf_op jit(solution)/shard_map/all_to_all | solution.py:98
  34.5 1.9 fusion.25
  37.2 4.1 scatter_custom_fusion
  41.3 4.6 reshape.101
  45.9 14.8 %all-to-all-start = ((bf16[64,1,9,2048]{3,2,1,0:T(8,128)(2,1)}), bf16[64,1,9,2048]{3,2,1,0:T(8,128)(2,1)}, u32[]{:S(2)}, u32[]{:S(2)}) async-start(bf16[64,1,9,2048]{3,2,1,0:T(8,128)(2,1)} %bitcast.69), calls=%async_computation | async-start | bytes 8388608 | tf_op jit(solution)/shard_map/all_to_all | solution.py:97
  61.0 183.4 %all-to-all-done = bf16[64,1,9,2048]{3,2,1,0:T(8,128)(2,1)} async-done(((bf16[64,1,9,2048]{3,2,1,0:T(8,128)(2,1)}), bf16[64,1,9,2048]{3,2,1,0:T(8,128)(2,1)}, u32[]{:S(2)}, u32[]{:S(2)}) %all-to-all-start) | async-done | bytes 2359328 | tf_op jit(solution)/shard_map/all_to_all | solution.py:97
  244.3 4.7 squeeze.14
  249.0 4.3 copy.24
  253.4 1.4 broadcast.108
  254.8 113.3 %while.24 = (s32[]{:T(128)}, bf16[576,1536]{0,1:T(8,128)(2,1)}, bf16[576,2048]{0,1:T(8,128)(2,1)}, pred[576]{0:T(1024)(128)(4,1)S(1)}, s32[]{:T(128)}, /*index=5...) while((s32[]{:T(128)}, bf16[576,1536]{0,1:T(8,128)(2,1)}, ...), condition=%wide.region_11.12_spmd.clone, body=%wide.region_7.11_spmd.clone.sunk | while | flops 260331856 | bytes 16045296 | solution.py:71
  258.4 1.4 fusion.90
  259.8 2.9 multiply_convert_fusion.3
  262.7 2.1 fusion.91
  264.7 2.1 fusion.92
  266.8 2.1 fusion.93
  268.9 1.4 fusion.87
  272.6 1.4 fusion.90
  274.0 2.9 multiply_convert_fusion.3
  276.9 2.0 fusion.91
  278.9 2.1 fusion.92
  281.0 2.1 fusion.93
  286.7 1.4 fusion.90
  288.2 2.9 multiply_convert_fusion.3
  291.0 2.1 fusion.91
  293.1 2.1 fusion.92
  295.2 2.1 fusion.93
  300.9 1.4 fusion.90
  302.3 2.9 multiply_convert_fusion.3
  305.2 2.0 fusion.91
  307.3 2.1 fusion.92
  309.4 2.1 fusion.93
  315.1 1.4 fusion.90
  316.5 2.9 multiply_convert_fusion.3
  319.4 2.0 fusion.91
  321.4 2.1 fusion.92
  323.5 2.1 fusion.93
  329.2 1.4 fusion.90
  330.7 2.9 multiply_convert_fusion.3
  333.5 2.1 fusion.91
  335.6 2.1 fusion.92
  337.7 2.1 fusion.93
  343.4 1.4 fusion.90
  344.8 2.9 multiply_convert_fusion.3
  347.7 2.1 fusion.91
  349.7 2.1 fusion.92
  351.8 2.1 fusion.93
  353.9 1.4 fusion.87
  357.6 1.4 fusion.90
  359.0 2.9 multiply_convert_fusion.3
  361.8 2.1 fusion.91
  363.9 2.1 fusion.92
  366.0 2.1 fusion.93
  368.1 3.9 copy.25
  372.0 4.2 transpose_reshape.3
  376.2 11.6 all-to-all-start.2
  388.1 137.9 %all-to-all-done.2 = bf16[64,1,9,1536]{3,2,1,0:T(8,128)(2,1)} async-done(((bf16[64,1,9,1536]{3,2,1,0:T(8,128)(2,1)}), bf16[64,1,9,1536]{3,2,1,0:T(8,128)(2,1)}, u32[]{:S(2)}, u32[]{:S(2)}) %all-to-all-start.2) | async-done | bytes 1769504 | tf_op jit(solution)/shard_map/all_to_all | solution.py:111
  526.0 4.2 reshape.103
  530.2 4.1 gather_fusion
  534.4 3.0 fusion.24
  538.6 17.6 %reduce-scatter.2.cloned.1.call-done = bf16[192,512]{1,0:T(8,128)(2,1)} async-done(((bf16[192,1024]{1,0:T(8,128)(2,1)}), bf16[192,512]{1,0:T(8,128)(2,1)}) %reduce-scatter.2.cloned.1.call-update) | async-done | bytes 196624 | tf_op jit(solution)/shard_map/reduce_scatter | solution.py:124
  557.6 579.8 %psum.23 = f32[512]{0:T(512)S(1)} all-reduce(f32[512]{0:T(512)S(1)} %get-tuple-element.173), channel_id=1, replica_groups=mesh['seq'=64,'head'=2,'dp'=4] {'seq','dp'}, use_global_device_ids=true, to_apply=%region_18.19 | all-reduce | flops 512 | bytes 4096 | tf_op jit(solution)/shard_map/psum | solution.py:141
  1138.0 112.8 %all-reduce.1 = (f32[192,1]{0,1:T(1,128)S(1)}, f32[192,1]{0,1:T(1,128)S(1)}) all-reduce(f32[192,1]{0,1:T(1,128)S(1)} %bitcast.76, f32[192,1]{0,1:T(1,128)S(1)} %bitcast.77), channel_id=1, replica_groups=mesh['seq'=64,'head'=2,'dp'=4] {'head'}, use_global_device_ids=true, to_apply=%region_16.17 | all-reduce | flops 384 | bytes 3072 | tf_op jit(solution)/shard_map/psum | solution.py:128
  1250.8 1.9 fusion.48
  (74 shorter events, 37.2 us)
Async XLA Ops:
  7.2 27.3 %copy-start = (bf16[3,1024,512]{2,1,0:T(8,128)(2,1)S(1)}, bf16[3,1024,512]{2,1,0:T(8,128)(2,1)}, u32[]{:S(2)}) copy-start(bf16[3,1024,512]{2,1,0:T(8,128)(2,1)} %param.9) | copy-start | bytes 9437188
  12.9 33.0 %all-to-all-start.1 = ((bf16[64,1,9]{2,1,0:T(2,128)(2,1)}), bf16[64,1,9]{2,1,0:T(2,128)(2,1)S(1)}, u32[]{:S(2)}, u32[]{:S(2)}) async-start(bf16[64,1,9]{2,1,0:T(2,128)(2,1)} %reshape.133), calls=%async_computation.1 | async-start | bytes 65536 | tf_op jit(solution)/shard_map/all_to_all | solution.py:98
  34.4 2.8 copy-start.3
  45.9 198.5 %all-to-all-start = ((bf16[64,1,9,2048]{3,2,1,0:T(8,128)(2,1)}), bf16[64,1,9,2048]{3,2,1,0:T(8,128)(2,1)}, u32[]{:S(2)}, u32[]{:S(2)}) async-start(bf16[64,1,9,2048]{3,2,1,0:T(8,128)(2,1)} %bitcast.69), calls=%async_computation | async-start | bytes 8388608 | tf_op jit(solution)/shard_map/all_to_all | solution.py:97
  256.1 1.2 copy-start.1
  270.3 1.2 copy-start.1
  284.5 1.2 copy-start.1
  298.7 1.2 copy-start.1
  312.8 1.2 copy-start.1
  327.0 1.2 copy-start.1
  341.1 1.2 copy-start.1
  355.3 1.2 copy-start.1
  376.2 149.7 %all-to-all-start.2 = ((bf16[64,1,9,1536]{3,2,1,0:T(8,128)(2,1)}), bf16[64,1,9,1536]{3,2,1,0:T(8,128)(2,1)}, u32[]{:S(2)}, u32[]{:S(2)}) async-start(bf16[64,1,9,1536]{3,2,1,0:T(8,128)(2,1)} %bitcast.70), calls=%async_computation.2 | async-start | bytes 6291456 | tf_op jit(solution)/shard_map/all_to_all | solution.py:111
  387.8 168.4 %reduce-scatter.2.cloned.1.call-start = ((), (), s32[]{:S(2)}) async-start(), calls=%async_computation.4 | async-start | bytes 589824 | tf_op jit(solution)/shard_map/reduce_scatter | solution.py:124
  534.4 3.1 copy-start.4
  534.4 3.1 copy-start.2
Sparse Core Ops, SparseCore 0:
  537.5 18.6 reduce-scatter.1
where the time goes:
time: 1260 us
  blocking collectives  693 us (55%)
  waiting for transfers between devices  339 us (27%)
  matrix products  99.9 us (8%)
  starting transfers between devices  45.7 us (4%)
  local copies, waits for them, and re-layouts  42.7 us (3%)
  other arithmetic  25.4 us (2%)
  between operations  14.2 us (1%)
    psum x1, blocking collectives, on_device(): gain_total = lax.psum(local_sum, ('seq', 'dp'))  580 us
    all_to_all x1, waiting for transfers between devices, on_device(): lax.all_to_all(outgoing, 'seq', split_axis=0, concat_axis=0, tiled=True)  183 us
    all_to_all x1, waiting for transfers between devices, on_device(): lax.all_to_all(answer, 'seq', split_axis=0, concat_axis=0, tiled=True)  138 us
    psum x1, blocking collectives, on_device(): lax.psum((jnp.sum(scaled_grad, -1, keepdims=True), jnp.sum(scaled_grad *...  113 us
  transfers between devices with their start and end apart: 4, of which 3 were waited for; matrix products, arithmetic and copies ran while one was open for 1% of the time, Pallas kernels for 0%

commit v1 on v0

--- a/solution.py
+++ b/solution.py
@@ -138,7 +138,7 @@
         jnp.bfloat16
     )
     local_sum = jnp.sum(gradient * own_scaled, 0)
-    gain_total = lax.psum(local_sum, ("seq", "dp"))
+    gain_total = lax.psum(lax.psum(local_sum, "dp"), "seq")
     gain_gradient = gain_total * (seq_count * lax.axis_size("dp") * tokens) ** (-0.5)
     return (input_gradient.reshape(1, tokens, half_width), gain_gradient)
 

time: 1260 us -> 725 us (0.58)
  blocking collectives: 693 us -> 156 us
    psum x1 -> x2, blocking collectives: 580 us -> 124 us  [on_device(): gain_total = lax.psum(lax.psum(local_sum, 'dp'), 'seq')]
    psum x1, blocking collectives: 113 us -> 32.4 us  [on_device(): lax.psum((jnp.sum(scaled_grad, -1, keepdims=True), jnp.sum(scaled_grad *...]
  transfers between devices with their start and end apart: 4 -> 4, of which waited for: 3 -> 3; matrix products, arithmetic and copies ran while one was open for 1% -> 2% of each run, Pallas kernels for 0% -> 0%
where the time goes in v1:
time: 725 us; the launch traced here: 723 us
  waiting for transfers between devices  339 us (47%)
  blocking collectives  156 us (22%)
  matrix products  99.9 us (14%)
  starting transfers between devices  45.7 us (6%)
  local copies, waits for them, and re-layouts  42.7 us (6%)
  other arithmetic  25.4 us (4%)
  between operations  14.2 us (2%)
    all_to_all x1, waiting for transfers between devices, on_device(): lax.all_to_all(outgoing, 'seq', split_axis=0, concat_axis=0, tiled=True)  183 us
    all_to_all x1, waiting for transfers between devices, on_device(): lax.all_to_all(answer, 'seq', split_axis=0, concat_axis=0, tiled=True)  138 us
    psum x2, blocking collectives, on_device(): gain_total = lax.psum(lax.psum(local_sum, 'dp'), 'seq')  124 us
    psum x1, blocking collectives, on_device(): lax.psum((jnp.sum(scaled_grad, -1, keepdims=True), jnp.sum(scaled_grad *...  32.4 us
    dot_general x8, matrix products, attend_backward(): lax.dot_general(upstream, values, (((1,), (1,)), ((), ())), preferred_ele...  22.9 us
    all_to_all x1, starting transfers between devices, on_device(): lax.all_to_all(present, 'seq', split_axis=0, concat_axis=0, tiled=True)  19.1 us
    reduce_scatter x1, waiting for transfers between devices, on_device(): lax.psum_scatter(partial_value.astype(jnp.bfloat16), 'head', scatter_dime...  17.6 us
    dot_general x8, matrix products, attend_backward(): lax.dot_general(grad_scores, queries, (((0,), (0,)), ((), ())), preferred...  16.8 us
  transfers between devices with their start and end apart: 4, of which 3 were waited for; matrix products, arithmetic and copies ran while one was open for 2% of the time, Pallas kernels for 0%

profile of v1, /device:TPU:1, one launch (start us, length us, event | category | flops | bytes accessed | tf_op | source)
XLA Modules:
  0.0 722.8 jit_solution(5572439720293014621)
XLA Ops:
  10.4 1.8 scatter_custom_fusion.1
  12.9 19.1 %all-to-all-start.1 = ((bf16[64,1,9]{2,1,0:T(2,128)(2,1)}), bf16[64,1,9]{2,1,0:T(2,128)(2,1)S(1)}, u32[]{:S(2)}, u32[]{:S(2)}) async-start(bf16[64,1,9]{2,1,0:T(2,128)(2,1)} %reshape.133), calls=%async_computation.1 | async-start | bytes 65536 | tf_op jit(solution)/shard_map/all_to_all | solution.py:98
  34.5 1.9 fusion.25
  37.2 4.1 scatter_custom_fusion
  41.3 4.6 reshape.101
  45.9 14.8 %all-to-all-start = ((bf16[64,1,9,2048]{3,2,1,0:T(8,128)(2,1)}), bf16[64,1,9,2048]{3,2,1,0:T(8,128)(2,1)}, u32[]{:S(2)}, u32[]{:S(2)}) async-start(bf16[64,1,9,2048]{3,2,1,0:T(8,128)(2,1)} %bitcast.69), calls=%async_computation | async-start | bytes 8388608 | tf_op jit(solution)/shard_map/all_to_all | solution.py:97
  61.0 183.4 %all-to-all-done = bf16[64,1,9,2048]{3,2,1,0:T(8,128)(2,1)} async-done(((bf16[64,1,9,2048]{3,2,1,0:T(8,128)(2,1)}), bf16[64,1,9,2048]{3,2,1,0:T(8,128)(2,1)}, u32[]{:S(2)}, u32[]{:S(2)}) %all-to-all-start) | async-done | bytes 2359328 | tf_op jit(solution)/shard_map/all_to_all | solution.py:97
  244.3 4.7 squeeze.14
  249.0 4.3 copy.24
  253.4 1.4 broadcast.108
  254.8 113.3 %while.24 = (s32[]{:T(128)}, bf16[576,1536]{0,1:T(8,128)(2,1)}, bf16[576,2048]{0,1:T(8,128)(2,1)}, pred[576]{0:T(1024)(128)(4,1)S(1)}, s32[]{:T(128)}, /*index=5...) while((s32[]{:T(128)}, bf16[576,1536]{0,1:T(8,128)(2,1)}, ...), condition=%wide.region_11.12_spmd.clone, body=%wide.region_7.11_spmd.clone.sunk | while | flops 260331856 | bytes 16045296 | solution.py:71
  258.4 1.4 fusion.90
  259.8 2.9 multiply_convert_fusion.3
  262.7 2.1 fusion.91
  264.7 2.1 fusion.92
  266.8 2.1 fusion.93
  268.9 1.4 fusion.87
  272.6 1.4 fusion.90
  274.0 2.9 multiply_convert_fusion.3
  276.9 2.0 fusion.91
  278.9 2.1 fusion.92
  281.0 2.1 fusion.93
  286.7 1.4 fusion.90
  288.2 2.9 multiply_convert_fusion.3
  291.0 2.1 fusion.91
  293.1 2.1 fusion.92
  295.2 2.1 fusion.93
  300.9 1.4 fusion.90
  302.3 2.9 multiply_convert_fusion.3
  305.2 2.0 fusion.91
  307.3 2.1 fusion.92
  309.4 2.1 fusion.93
  315.1 1.4 fusion.90
  316.5 2.9 multiply_convert_fusion.3
  319.4 2.0 fusion.91
  321.4 2.1 fusion.92
  323.5 2.1 fusion.93
  329.2 1.4 fusion.90
  330.7 2.9 multiply_convert_fusion.3
  333.5 2.1 fusion.91
  335.6 2.1 fusion.92
  337.7 2.1 fusion.93
  343.4 1.4 fusion.90
  344.8 2.9 multiply_convert_fusion.3
  347.7 2.1 fusion.91
  349.7 2.1 fusion.92
  351.8 2.1 fusion.93
  357.6 1.4 fusion.90
  359.0 2.9 multiply_convert_fusion.3
  361.8 2.1 fusion.91
  363.9 2.1 fusion.92
  366.0 2.1 fusion.93
  368.1 3.9 copy.25
  372.0 4.2 transpose_reshape.3
  376.2 11.6 %all-to-all-start.2 = ((bf16[64,1,9,1536]{3,2,1,0:T(8,128)(2,1)}), bf16[64,1,9,1536]{3,2,1,0:T(8,128)(2,1)}, u32[]{:S(2)}, u32[]{:S(2)}) async-start(bf16[64,1,9,1536]{3,2,1,0:T(8,128)(2,1)} %bitcast.70), calls=%async_computation.2 | async-start | bytes 6291456 | tf_op jit(solution)/shard_map/all_to_all | solution.py:111
  388.1 137.9 %all-to-all-done.2 = bf16[64,1,9,1536]{3,2,1,0:T(8,128)(2,1)} async-done(((bf16[64,1,9,1536]{3,2,1,0:T(8,128)(2,1)}), bf16[64,1,9,1536]{3,2,1,0:T(8,128)(2,1)}, u32[]{:S(2)}, u32[]{:S(2)}) %all-to-all-start.2) | async-done | bytes 1769504 | tf_op jit(solution)/shard_map/all_to_all | solution.py:111
  526.0 4.2 reshape.103
  530.2 4.1 gather_fusion
  534.4 3.0 fusion.24
  538.6 17.6 %reduce-scatter.2.cloned.1.call-done = bf16[192,512]{1,0:T(8,128)(2,1)} async-done(((bf16[192,1024]{1,0:T(8,128)(2,1)}), bf16[192,512]{1,0:T(8,128)(2,1)}) %reduce-scatter.2.cloned.1.call-update) | async-done | bytes 196624 | tf_op jit(solution)/shard_map/reduce_scatter | solution.py:124
  557.6 7.4 %psum.30 = f32[512]{0:T(512)S(1)} all-reduce(f32[512]{0:T(512)S(1)} %get-tuple-element.173), channel_id=1, replica_groups=mesh['seq'=64,'head'=2,'dp'=4] {'dp'}, use_global_device_ids=true, to_apply=%region_18.19 | all-reduce | flops 512 | bytes 4096 | tf_op jit(solution)/shard_map/psum | solution.py:141
  565.0 116.1 %psum.31 = f32[512]{0:T(512)S(1)} all-reduce(f32[512]{0:T(512)S(1)} %psum.30), channel_id=1, replica_groups=mesh['seq'=64,'head'=2,'dp'=4] {'seq'}, use_global_device_ids=true, to_apply=%region_19.20 | all-reduce | flops 512 | bytes 4096 | tf_op jit(solution)/shard_map/psum | solution.py:141
  681.7 32.4 %all-reduce.1 = (f32[192,1]{0,1:T(1,128)S(1)}, f32[192,1]{0,1:T(1,128)S(1)}) all-reduce(f32[192,1]{0,1:T(1,128)S(1)} %bitcast.76, f32[192,1]{0,1:T(1,128)S(1)} %bitcast.77), channel_id=1, replica_groups=mesh['seq'=64,'head'=2,'dp'=4] {'head'}, use_global_device_ids=true, to_apply=%region_16.17 | all-reduce | flops 384 | bytes 3072 | tf_op jit(solution)/shard_map/psum | solution.py:128
  714.1 1.9 fusion.48
  (75 shorter events, 38.5 us)
Async XLA Ops:
  7.2 27.3 %copy-start = (bf16[3,1024,512]{2,1,0:T(8,128)(2,1)S(1)}, bf16[3,1024,512]{2,1,0:T(8,128)(2,1)}, u32[]{:S(2)}) copy-start(bf16[3,1024,512]{2,1,0:T(8,128)(2,1)} %param.9) | copy-start | bytes 9437188
  12.9 33.0 %all-to-all-start.1 = ((bf16[64,1,9]{2,1,0:T(2,128)(2,1)}), bf16[64,1,9]{2,1,0:T(2,128)(2,1)S(1)}, u32[]{:S(2)}, u32[]{:S(2)}) async-start(bf16[64,1,9]{2,1,0:T(2,128)(2,1)} %reshape.133), calls=%async_computation.1 | async-start | bytes 65536 | tf_op jit(solution)/shard_map/all_to_all | solution.py:98
  34.4 2.8 copy-start.3
  45.9 198.5 %all-to-all-start = ((bf16[64,1,9,2048]{3,2,1,0:T(8,128)(2,1)}), bf16[64,1,9,2048]{3,2,1,0:T(8,128)(2,1)}, u32[]{:S(2)}, u32[]{:S(2)}) async-start(bf16[64,1,9,2048]{3,2,1,0:T(8,128)(2,1)} %bitcast.69), calls=%async_computation | async-start | bytes 8388608 | tf_op jit(solution)/shard_map/all_to_all | solution.py:97
  256.1 1.2 copy-start.1
  270.3 1.2 copy-start.1
  284.5 1.2 copy-start.1
  298.7 1.2 copy-start.1
  312.8 1.2 copy-start.1
  327.0 1.2 copy-start.1
  341.1 1.2 copy-start.1
  355.3 1.2 copy-start.1
  376.2 149.7 %all-to-all-start.2 = ((bf16[64,1,9,1536]{3,2,1,0:T(8,128)(2,1)}), bf16[64,1,9,1536]{3,2,1,0:T(8,128)(2,1)}, u32[]{:S(2)}, u32[]{:S(2)}) async-start(bf16[64,1,9,1536]{3,2,1,0:T(8,128)(2,1)} %bitcast.70), calls=%async_computation.2 | async-start | bytes 6291456 | tf_op jit(solution)/shard_map/all_to_all | solution.py:111
  387.8 168.4 %reduce-scatter.2.cloned.1.call-start = ((), (), s32[]{:S(2)}) async-start(), calls=%async_computation.4 | async-start | bytes 589824 | tf_op jit(solution)/shard_map/reduce_scatter | solution.py:124
  534.4 3.1 copy-start.4
  534.4 3.1 copy-start.2
Sparse Core Ops, SparseCore 0:
  537.5 18.6 reduce-scatter.1
